TPU v7x, 32 devices: a whole 2x2x4 slice. The times are simulated.
32 devices in a mesh: comp: 4 (over y, core), tp: 8 (over z, x).
Axes of the slice: x: 2, y: 2, z: 4, core: 2. Of those that a mesh axis runs over, the one named last changes fastest.
Arguments:
- queries: bfloat16 [4, 512, 1024], P('comp', None, 'tp'), may hold values from -8 to 8
- answer_keys: bfloat16 [4, 512, 128], P('comp'), may hold values from -6 to 6
- answer_values: bfloat16 [4, 512, 128], P('comp'), may hold values from -6 to 6
- prompt_keys: bfloat16 [768, 128], P('comp'), may hold values from -8 to 8
- prompt_values: bfloat16 [768, 128], P('comp'), may hold values from -6 to 6
- out_grad: bfloat16 [4, 512, 1024], P('comp', None, 'tp'), may hold values from -6 to 6
- block_counts: int32 [4], replicated, may hold values from 1 to 8, 18 in all
Outputs:
- attended: bfloat16 [4, 512, 1024], P('comp', None, 'tp')
- query_grad: bfloat16 [4, 512, 1024], P('comp', None, 'tp')
- keygrad_prompt: bfloat16 [768, 128], P('comp')
- valgrad_prompt: bfloat16 [768, 128], P('comp')
- keygrad_answer: bfloat16 [4, 512, 128], P('comp')
- valgrad_answer: bfloat16 [4, 512, 128], P('comp')
Inputs may be any that keep to these rules, and one draw needn't show every extreme that they name: `block_counts`: the counts add up to 18; the largest is 8.
All inputs are finite; a program needn't handle non-finite values.
Results may differ from a plain program's by a relative error of at most 0.012.
Values may be sent and summed in bfloat16 or wider, within the bound.
A program may use at most 64 MiB of HBM per device.

v0:
```python
import jax
import jax.numpy as jnp
from jax import lax
from jax.sharding import PartitionSpec as P

GROUP = 8
BLK = 64


NEG = -1e30


def contract(left, right, left_dim, right_dim):
    return lax.dot_general(
        left, right, (((left_dim,), (right_dim,)), ((), ())), preferred_element_type=jnp.float32
    )


def shards(queries, answer_keys, answer_values, prompt_keys, prompt_values, out_grad, block_counts):
    head_dim = queries.shape[2]
    length = queries.shape[1]
    kv_width = prompt_keys.shape[1]
    factor = head_dim ** (-0.5)
    comp_index = lax.axis_index("comp")
    kv_group = lax.axis_index("tp") // GROUP
    row_counts = block_counts * BLK
    completions = row_counts.shape[0]
    own_count = jnp.sum(jnp.where(jnp.arange(completions) == comp_index, row_counts, 0))
    positions = jnp.arange(length)
    active = positions < own_count
    query_own = queries[0]
    dout_own = out_grad[0] * active[:, None].astype(jnp.bfloat16)
    key_self = lax.dynamic_slice_in_dim(answer_keys[0], kv_group * head_dim, head_dim, 1)
    value_self = lax.dynamic_slice_in_dim(answer_values[0], kv_group * head_dim, head_dim, 1)
    key_mine = lax.dynamic_slice_in_dim(prompt_keys, kv_group * head_dim, head_dim, 1)
    value_mine = lax.dynamic_slice_in_dim(prompt_values, kv_group * head_dim, head_dim, 1)
    score_self = jnp.where(
        positions[None, :] <= positions[:, None], contract(query_own, key_self, 1, 1) * factor, NEG
    )
    key_all, value_all = (
        lax.all_gather(key_mine, "comp", axis=0, tiled=True),
        lax.all_gather(value_mine, "comp", axis=0, tiled=True),
    )
    score_prompt = contract(query_own, key_all, 1, 1) * factor
    peak = jnp.maximum(score_prompt.max(1), score_self.max(1))
    summed = jnp.sum(jnp.exp(score_prompt - peak[:, None]), 1) + jnp.sum(
        jnp.exp(score_self - peak[:, None]), 1
    )
    log_total = peak + jnp.log(summed)
    prob_prompt = jnp.exp(score_prompt - log_total[:, None])
    rounded_prompt = prob_prompt.astype(jnp.bfloat16)
    prob_self = jnp.exp(score_self - log_total[:, None])
    rounded_self = prob_self.astype(jnp.bfloat16)
    mixed = jnp.dot(rounded_prompt, value_all, preferred_element_type=jnp.float32) + jnp.dot(
        rounded_self, value_self, preferred_element_type=jnp.float32
    )
    attended = (mixed * active[:, None].astype(jnp.float32)).astype(jnp.bfloat16)
    delta_row = jnp.sum(dout_own.astype(jnp.float32) * attended.astype(jnp.float32), 1)
    dscore_prompt = prob_prompt * (contract(dout_own, value_all, 1, 1) - delta_row[:, None])
    scaled_prompt = (dscore_prompt * factor).astype(jnp.bfloat16)
    grad_prompt = jnp.dot(scaled_prompt, key_all, preferred_element_type=jnp.float32)
    prompt_terms = (
        contract(scaled_prompt, query_own, 0, 0),
        contract(rounded_prompt, dout_own, 0, 0),
    )
    key_part, value_term = (
        lax.psum_scatter(prompt_terms[0], "comp", scatter_dimension=0, tiled=True),
        lax.psum_scatter(prompt_terms[1], "comp", scatter_dimension=0, tiled=True),
    )
    dscore_self = prob_self * (contract(dout_own, value_self, 1, 1) - delta_row[:, None])
    scaled_self = (dscore_self * factor).astype(jnp.bfloat16)
    query_grad = (
        grad_prompt + jnp.dot(scaled_self, key_self, preferred_element_type=jnp.float32)
    ).astype(jnp.bfloat16)
    answer_key_term = contract(scaled_self, query_own, 0, 0)
    answer_value_term = contract(rounded_self, dout_own, 0, 0)

    def embed_head(part):
        holder = jnp.zeros((part.shape[0], kv_width), jnp.float32)
        return lax.dynamic_update_slice_in_dim(holder, part, kv_group * head_dim, 1)

    group_totals = lax.psum(
        (
            embed_head(key_part),
            embed_head(value_term),
            embed_head(answer_key_term),
            embed_head(answer_value_term),
        ),
        "tp",
    )
    key_total = group_totals[0].astype(jnp.bfloat16)
    value_total = group_totals[1].astype(jnp.bfloat16)
    answer_key_total = group_totals[2].astype(jnp.bfloat16)
    answer_value_total = group_totals[3].astype(jnp.bfloat16)
    return (
        attended[None],
        query_grad[None],
        key_total,
        value_total,
        answer_key_total[None],
        answer_value_total[None],
    )


def solution(mesh):
    return jax.shard_map(
        shards,
        mesh=mesh,
        in_specs=(
            P("comp", None, "tp"),
            P("comp", None, None),
            P("comp", None, None),
            P("comp", None),
            P("comp", None),
            P("comp", None, "tp"),
            P(),
        ),
        out_specs=(
            P("comp", None, "tp"),
            P("comp", None, "tp"),
            P("comp", None),
            P("comp", None),
            P("comp", None, None),
            P("comp", None, None),
        ),
        check_vma=False,
    )
```

profile of v0, /device:TPU:0, one launch (start us, length us, event | category | flops | bytes accessed | tf_op | source)
XLA Modules:
  0.0 119.1 jit_solution(13426869620118113481)
XLA Ops:
  7.2 0.0 copy-start
  7.2 0.0 reduce-scatter.5.cloned.1.call-start
  7.2 1.3 %fusion.32 = s32[]{:T(128)} fusion(s32[4]{0:T(128)} %param.13, s32[]{:T(128)S(6)} %axis_index.19), kind=kLoop, calls=%fused_computation.48 | loop fusion | flops 15 | bytes 24 | tf_op jit(solution)/shard_map/reduce_sum | solution.py:28
  8.6 0.6 fusion.30
  9.2 1.0 copy.13
  10.2 0.0 copy-start.1
  10.2 7.1 %all_gather.6 = bf16[768,128]{1,0:T(8,128)(2,1)S(1)} all-gather(bf16[192,128]{1,0:T(8,128)(2,1)} %param.10), channel_id=1, replica_groups=mesh['comp'=4,'tp'=8] {'comp'}, dimensions={0}, use_global_device_ids=true | all-gather | bytes 245760 | tf_op jit(solution)/shard_map/all_gather | solution.py:41
  17.3 1.3 %fusion.37 = (f32[512]{0:T(512)S(1)}, f32[512,512]{0,1:T(8,128)S(1)}) fusion(bf16[1,512,128]{2,1,0:T(8,128)(2,1)} %param.8, bf16[1,512,128]{2,1,0:T(8,128)(2,1)S(1)} %copy-done), kind=kOutput, calls=%fused_computation.51 | convolution fusion | flops 68156928 | bytes 1312768 | tf_op jit(solution)/shard_map/dot_general | solution.py:14
  18.6 0.5 fusion.36
  19.1 0.2 exponential_reduce_fusion.1
  19.3 0.4 exponential_reduce_fusion
  19.7 1.3 %fusion.25 = f32[768,128]{1,0:T(8,128)} fusion(bf16[1,512,128]{1,2,0:T(8,128)(2,1)S(1)} %copy.13, bf16[512]{0:T(512)(128)(2,1)S(1)} %fusion.30, f32[512,768]{1,0:T(8,128)S(1)} %get-tuple-element.17, f32[512]{0:T(512)S(1)} %log_add_fusion), kind=kOutput, calls=%fused_computation.38 | convolution fusion | flops 101515264 | bytes 2100224 | tf_op jit(solution)/shard_map/dot_general | solution.py:14
  21.0 0.0 reduce-scatter.5.cloned.1.call-update
  21.1 0.0 reduce-scatter.3.cloned.1.call-start
  21.1 0.7 fusion.31
  21.8 5.6 %all_gather.7 = bf16[768,128]{1,0:T(8,128)(2,1)S(1)} all-gather(bf16[192,128]{1,0:T(8,128)(2,1)S(1)} %copy-done.10), channel_id=1, replica_groups=mesh['comp'=4,'tp'=8] {'comp'}, dimensions={0}, use_global_device_ids=true | all-gather | bytes 245760 | tf_op jit(solution)/shard_map/all_gather | solution.py:42
  27.4 0.6 fusion.34
  28.0 1.0 multiply_reduce_fusion
  29.0 1.5 %multiply_convert_fusion = bf16[512,768]{1,0:T(8,128)(2,1)S(1)} fusion(bf16[768,128]{1,0:T(8,128)(2,1)S(1)} %all_gather.7, f32[512,768]{1,0:T(8,128)S(1)} %get-tuple-element.17, f32[512]{0:T(512)S(1)} %get-tuple-element.20, f32[512]{0:T(512)S(1)} %log_add_fusion, bf16[1,512,128]{1,2,0:T(8,128)(2,1)} %copy-done.1, bf16[512]{0:T(512)(128)(2,1)S(1)} %fusion.30), kind=kOutput, calls=%fused_computation | convolution fusion | flops 102694912 | bytes 2692096 | tf_op jit(solution)/shard_map/dot_general | solution.py:14
  30.5 0.0 copy-start.2
  30.5 1.2 fusion.20
  31.7 0.0 reduce-scatter.3.cloned.1.call-update
  31.7 0.4 fusion.4
  32.2 0.3 fusion.10
  32.5 0.1 copy-done.8
  32.6 0.8 copy.15
  33.4 0.3 fusion.18
  33.7 0.4 fusion.38
  34.1 1.0 fusion.8
  35.1 8.4 %reduce-scatter.5.cloned.1.call-done = f32[192,128]{1,0:T(8,128)} async-done(((f32[768,128]{1,0:T(8,128)}), f32[192,128]{1,0:T(8,128)}) %reduce-scatter.5.cloned.1.call-update) | async-done | bytes 98320 | tf_op jit(solution)/shard_map/reduce_scatter | solution.py:68
  43.5 23.4 %reduce-scatter.3.cloned.1.call-done = f32[192,128]{1,0:T(8,128)} async-done(((f32[768,128]{1,0:T(8,128)}), f32[192,128]{1,0:T(8,128)}) %reduce-scatter.3.cloned.1.call-update) | async-done | bytes 98320 | tf_op jit(solution)/shard_map/reduce_scatter | solution.py:67
  66.9 45.4 %all-reduce.2 = (bf16[192,128]{1,0:T(8,128)(2,1)}, bf16[192,128]{1,0:T(8,128)(2,1)}, bf16[512,128]{1,0:T(8,128)(2,1)}, bf16[512,128]{1,0:T(8,128)(2,1)}) all-reduce(f32[192,128]{1,0:T(8,128)} %reduce-scatter.3.cloned.1.call-done, f32[192,128]{1,0:T(8,128)} %reduce-scatter.5.cloned.1.call-done, ...), channel_id=1, replica_groups=mesh['comp'=4,'tp'=8] {'tp'}, use_global_device_ids=true, to_apply=%region_7.8 | all-reduce | flops 180224 | bytes 1081344 | tf_op jit(solution)/shard_map/psum | solution.py:82
  (20 shorter events, 0.1 us)
Async XLA Ops:
  7.2 10.2 %copy-start = (bf16[1,512,128]{2,1,0:T(8,128)(2,1)S(1)}, bf16[1,512,128]{2,1,0:T(8,128)(2,1)}, u32[]{:S(2)}) copy-start(bf16[1,512,128]{2,1,0:T(8,128)(2,1)} %param.7) | copy-start | bytes 393220
  7.2 36.3 %reduce-scatter.5.cloned.1.call-start = ((), (), s32[]{:S(2)}) async-start(), calls=%async_computation.3 | async-start | bytes 491520 | tf_op jit(solution)/shard_map/reduce_scatter | solution.py:68
  10.2 17.8 %copy-start.1 = (bf16[1,512,128]{1,2,0:T(8,128)(2,1)}, bf16[1,512,128]{1,2,0:T(8,128)(2,1)S(1)}, u32[]{:S(2)}) copy-start(bf16[1,512,128]{1,2,0:T(8,128)(2,1)S(1)} %copy.13) | copy-start | bytes 393220
  17.3 1.8 %copy-start.3 = (bf16[768,128]{1,0:T(8,128)(2,1)}, bf16[768,128]{1,0:T(8,128)(2,1)S(1)}, u32[]{:S(2)}) copy-start(bf16[768,128]{1,0:T(8,128)(2,1)S(1)} %all_gather.6) | copy-start | bytes 589828
  19.7 2.1 %copy-start.10 = (bf16[192,128]{1,0:T(8,128)(2,1)S(1)}, bf16[192,128]{1,0:T(8,128)(2,1)}, u32[]{:S(2)}) copy-start(bf16[192,128]{1,0:T(8,128)(2,1)} %param.11) | copy-start | bytes 147460
  21.0 7.0 %copy-start.5 = (bf16[1,512,128]{2,1,0:T(8,128)(2,1)S(1)}, bf16[1,512,128]{2,1,0:T(8,128)(2,1)}, u32[]{:S(2)}) copy-start(bf16[1,512,128]{2,1,0:T(8,128)(2,1)} %param.9) | copy-start | bytes 393220
  21.1 45.8 %reduce-scatter.3.cloned.1.call-start = ((), (), s32[]{:S(2)}) async-start(), calls=%async_computation.2 | async-start | bytes 491520 | tf_op jit(solution)/shard_map/reduce_scatter | solution.py:67
  30.5 1.2 %copy-start.6 = (bf16[1,512,128]{2,1,0:T(8,128)(2,1)S(1)}, bf16[1,512,128]{2,1,0:T(8,128)(2,1)}, u32[]{:S(2)}) copy-start(bf16[1,512,128]{2,1,0:T(8,128)(2,1)} %param.9) | copy-start | bytes 393220
  30.5 1.2 %copy-start.7 = (bf16[1,512,128]{2,1,0:T(8,128)(2,1)S(1)}, bf16[1,512,128]{2,1,0:T(8,128)(2,1)}, u32[]{:S(2)}) copy-start(bf16[1,512,128]{2,1,0:T(8,128)(2,1)} %param.12) | copy-start | bytes 393220
  30.5 1.7 %copy-start.2 = (bf16[1,512,128]{1,2,0:T(8,128)(2,1)S(1)}, bf16[1,512,128]{1,2,0:T(8,128)(2,1)}, u32[]{:S(2)}) copy-start(bf16[1,512,128]{1,2,0:T(8,128)(2,1)} %copy-done.1) | copy-start | bytes 393220
  31.7 0.9 copy-start.8
  32.2 1.5 %copy-start.4 = (bf16[768,128]{1,0:T(8,128)(2,1)S(1)}, bf16[768,128]{1,0:T(8,128)(2,1)}, u32[]{:S(2)}) copy-start(bf16[768,128]{1,0:T(8,128)(2,1)} %copy-done.3) | copy-start | bytes 589828
  32.5 1.6 %copy-start.9 = (bf16[1,512,128]{2,1,0:T(8,128)(2,1)S(1)}, bf16[1,512,128]{2,1,0:T(8,128)(2,1)}, u32[]{:S(2)}) copy-start(bf16[1,512,128]{2,1,0:T(8,128)(2,1)} %param.8) | copy-start | bytes 393220
Sparse Core Ops, SparseCore 0:
  21.2 22.2 reduce-scatter.4
  46.0 20.8 reduce-scatter.2
where the time goes:
time: 119 us
  blocking collectives  58.1 us (49%)
  waiting for transfers between devices  31.8 us (27%)
  between operations  14.3 us (12%)
  matrix products  9.72 us (8%)
  other arithmetic  3.22 us (3%)
  local copies, waits for them, and re-layouts  1.92 us (2%)
    psum x1, blocking collectives, shards(): lax.psum((embed_head(key_part), embed_head(value_term), embed_head(answer...  45.4 us
    reduce_scatter x1, waiting for transfers between devices, shards(): lax.psum_scatter(prompt_terms[0], 'comp', scatter_dimension=0, tiled=True)  23.4 us
    reduce_scatter x1, waiting for transfers between devices, shards(): lax.psum_scatter(prompt_terms[1], 'comp', scatter_dimension=0, tiled=True)  8.43 us
    all_gather x1, blocking collectives, shards(): lax.all_gather(key_mine, 'comp', axis=0, tiled=True)  7.08 us
    dot_general x8, matrix products, contract(): lax.dot_general(left, right, (((left_dim,), (right_dim,)), ((), ())), pre...  6.77 us
    all_gather x1, blocking collectives, shards(): lax.all_gather(value_mine, 'comp', axis=0, tiled=True)  5.61 us
  transfers between devices with their start and end apart: 2, of which 2 were waited for; matrix products, arithmetic and copies ran while one was open for 7% of the time, Pallas kernels for 0%

commit v1 on v0

v1 whole, which is shorter than its diff:
```python
import functools
import jax
import jax.numpy as jnp
from jax import lax
from jax.experimental import pallas as pl
from jax.experimental.pallas import tpu as pltpu
from jax.sharding import PartitionSpec as P

GROUP = 8
BLK = 64
QUAD = 4
COLS = 256
NEG = -1e30
MESH = pl.DeviceIdType.MESH


def contract(left, right, left_dim, right_dim):
    return lax.dot_general(
        left, right, (((left_dim,), (right_dim,)), ((), ())), preferred_element_type=jnp.float32
    )


def kernel(
    n, q_ref, ka_ref, va_ref, kp_ref, vp_ref, do_ref, cnt_ref,
    att_ref, dq_ref, gp_ref, ga_ref,
    k_all, v_all, do_m, st, pb, dsb,
    pown, psend, precv, aown, asend, arecv,
    pxown, pxsend, pxrecv, pzown, pzsend, pzrecv, azown, azsend, azrecv,
    send_sem, recv_sem,
):
    me = lax.axis_index("comp")
    tp = lax.axis_index("tp")
    local = lax.rem(tp, GROUP)
    base = tp - local
    par = lax.rem(local, 2)
    zi = local // 2
    length, hd = q_ref.shape
    shard = kp_ref.shape[0]
    prompt = n * shard
    factor = hd ** (-0.5)
    blocks = length // COLS
    partner = {"tp": base + local + 1 - 2 * par}
    quad = [None] + [{"tp": base + 2 * lax.rem(zi + e, QUAD) + par} for e in range(1, QUAD)]
    comp_to = [None] + [{"comp": lax.rem(me + d, n)} for d in range(1, n)]
    comp_back = [None] + [{"comp": lax.rem(me + n - d, n)} for d in range(1, n)]
    zsrc = [lax.rem(zi + QUAD - e, QUAD) for e in range(QUAD)]

    barrier = pltpu.get_barrier_semaphore()
    peers = comp_to[1:] + [partner] + quad[1:]
    for peer in peers:
        pl.semaphore_signal(barrier, inc=1, device_id=peer, device_id_type=MESH)

    count = [0]
    started = []

    def copy(src, dst, device):
        s = count[0]
        count[0] += 1
        c = pltpu.make_async_remote_copy(
            src_ref=src, dst_ref=dst, send_sem=send_sem.at[s], recv_sem=recv_sem.at[s],
            device_id=device, device_id_type=MESH,
        )
        started.append(c)
        return c

    pl.semaphore_wait(barrier, len(peers))

    k_in, v_in = [], []
    for d in range(1, n):
        k_in.append(copy(kp_ref, k_all.at[pl.ds(d * shard, shard)], comp_to[d]))
        k_in[-1].start()
    for d in range(1, n):
        v_in.append(copy(vp_ref, v_all.at[pl.ds(d * shard, shard)], comp_to[d]))
        v_in[-1].start()

    k_all[:shard] = kp_ref[...]
    k_all[prompt:] = ka_ref[...]
    v_all[:shard] = vp_ref[...]
    v_all[prompt:] = va_ref[...]
    own_count = cnt_ref[me] * BLK
    row = lax.broadcasted_iota(jnp.int32, (length, hd), 0)
    do_m[...] = jnp.where(row < own_count, do_ref[...].astype(jnp.float32), 0.0).astype(jnp.bfloat16)

    def cols(b):
        return slice(b * COLS, (b + 1) * COLS)

    def spans(b):
        return [(d * shard, shard) for d in range(n)] + [(prompt + a * COLS, COLS) for a in range(b + 1)]

    peaks = [None] * blocks

    def scores(b, at, size):
        s = contract(k_all[at:at + size], q_ref[cols(b)], 1, 1) * factor
        if at == prompt + b * COLS:
            m = lax.broadcasted_iota(jnp.int32, s.shape, 0)
            i = lax.broadcasted_iota(jnp.int32, s.shape, 1)
            s = jnp.where(m <= i, s, NEG)
        st[at:at + size, cols(b)] = s
        top = jnp.max(s, axis=0, keepdims=True)
        peaks[b] = top if peaks[b] is None else jnp.maximum(peaks[b], top)

    for b in range(blocks):
        for a in range(b + 1):
            scores(b, prompt + a * COLS, COLS)
        scores(b, 0, shard)
    for d in range(1, n):
        k_in[d - 1].wait_recv()
        for b in range(blocks):
            scores(b, d * shard, shard)

    for b in range(blocks):
        total = jnp.zeros((1, COLS), jnp.float32)
        for at, size in spans(b):
            e = jnp.exp(st[at:at + size, cols(b)] - peaks[b])
            st[at:at + size, cols(b)] = e
            total = total + jnp.sum(e, axis=0, keepdims=True)
        inv = 1.0 / total
        for at, size in spans(b):
            p = st[at:at + size, cols(b)] * inv
            st[at:at + size, cols(b)] = p
            pb[at:at + size, cols(b)] = p.astype(jnp.bfloat16)

    p_in = [[None] * n, [None] * n]

    def prompt_terms(w, probs, right):
        for d in range(n):
            g = jnp.dot(probs[d * shard:(d + 1) * shard], right[...], preferred_element_type=jnp.float32)
            if d == 0:
                pown[w] = g
            else:
                psend[w, d - 1] = g.astype(jnp.bfloat16)
                p_in[w][d] = copy(psend.at[w, d - 1], precv.at[w, d - 1], comp_back[d])
                p_in[w][d].start()

    half = length // 2
    quarter = half // QUAD
    a_in = [None, None]

    def answer_terms(w, probs, right):
        for a in range(blocks):
            at = prompt + a * COLS
            g = jnp.dot(
                probs[at:at + COLS, a * COLS:], right[a * COLS:], preferred_element_type=jnp.float32
            ).reshape(COLS * 2 // length, half, hd)
            first = a * COLS // half
            aown[w, first:first + g.shape[0]] = g
            asend[w, first:first + g.shape[0]] = g.astype(jnp.bfloat16)
        a_in[w] = copy(asend.at[w, 1 - par], arecv.at[w], partner)
        a_in[w].start()

    prompt_terms(1, pb, do_m)
    answer_terms(1, pb, do_m)

    for c in v_in:
        c.wait_recv()
    deltas = []
    for b in range(blocks):
        keys = prompt + (b + 1) * COLS
        mixed = contract(v_all[:keys], pb[:keys, cols(b)], 0, 0)
        lane = lax.broadcasted_iota(jnp.int32, mixed.shape, 1) + b * COLS
        mixed = jnp.where(lane < own_count, mixed, 0.0).astype(jnp.bfloat16).astype(jnp.float32)
        att_ref[cols(b)] = mixed.T.astype(jnp.bfloat16)
        dout_t = do_m[cols(b)].astype(jnp.float32).T
        deltas.append(jnp.sum(dout_t * mixed, axis=0, keepdims=True))

    for b in range(blocks):
        for at, size in spans(b):
            dp = contract(v_all[at:at + size], do_m[cols(b)], 1, 1)
            ds = st[at:at + size, cols(b)] * (dp - deltas[b]) * factor
            dsb[at:at + size, cols(b)] = ds.astype(jnp.bfloat16)

    prompt_terms(0, dsb, q_ref)
    answer_terms(0, dsb, q_ref)

    def quad_scatter(total, own, send, recv):
        size = recv.shape[1]
        own[...] = total.reshape(QUAD, size, hd)
        send[...] = total.astype(jnp.bfloat16).reshape(QUAD, size, hd)
        out = []
        for e in range(1, QUAD):
            c = copy(send.at[lax.rem(zi + e, QUAD)], recv.at[e - 1], quad[e])
            c.start()
            out.append(c)
        return out

    def quad_gather(copies, own, recv, out):
        total = own[zi]
        for e in range(1, QUAD):
            copies[e - 1].wait_recv()
            total = total + recv[e - 1].astype(jnp.float32)
        out[zi] = total.astype(jnp.bfloat16)
        zs = []
        for e in range(1, QUAD):
            c = copy(out.at[zi], out.at[zi], quad[e])
            c.start()
            zs.append(c)
        return zs

    waits = []

    def landed(c, ref):
        pltpu.make_async_remote_copy(
            src_ref=ref, dst_ref=ref, send_sem=c[1], recv_sem=c[2], device_id=partner, device_id_type=MESH
        ).wait_recv()

    def finish_start(mine):
        s = count[0]
        c = copy(mine.at[zi], mine.at[zi], partner)
        c.start()
        return s

    def finish_forward(first, zs, mine):
        for e in range(1, QUAD):
            landed((None, send_sem.at[zs[e - 1]], recv_sem.at[zs[e - 1]]), mine.at[zsrc[e]])
            c = copy(mine.at[zsrc[e]], mine.at[zsrc[e]], partner)
            c.start()

    def answer_scatter(w):
        a_in[w].wait_recv()
        return quad_scatter(
            aown[w, par] + arecv[w].astype(jnp.float32), azown.at[w], azsend.at[w], azrecv.at[w]
        )

    av = answer_scatter(1)
    for b in range(blocks):
        keys = prompt + (b + 1) * COLS
        dq = contract(k_all[:keys], dsb[:keys, cols(b)], 0, 0)
        dq_ref[cols(b)] = dq.T.astype(jnp.bfloat16)

    for w in (1, 0):
        total = pown[w]
        for d in range(1, n):
            p_in[w][d].wait_recv()
            total = total + precv[w, d - 1].astype(jnp.float32)
        pxown[w] = total
        pxsend[w] = total.astype(jnp.bfloat16)
    p_x = copy(pxsend.at[1 - par], pxrecv, partner)
    p_x.start()
    ak = answer_scatter(0)
    p_x.wait_recv()
    ap = quad_scatter(pxown[par] + pxrecv[...].astype(jnp.float32), pzown, pzsend, pzrecv)

    chunks = [
        (av, azown.at[1], azrecv.at[1], ga_ref.at[1, par], ga_ref.at[1, 1 - par]),
        (ak, azown.at[0], azrecv.at[0], ga_ref.at[0, par], ga_ref.at[0, 1 - par]),
        (ap, pzown, pzrecv, gp_ref.at[par], gp_ref.at[1 - par]),
    ]
    state = []
    for copies, own, recv, mine, other in chunks:
        z0 = count[0]
        quad_gather(copies, own, recv, mine)
        x0 = finish_start(mine)
        state.append((z0, x0))
    forwards = []
    for (copies, own, recv, mine, other), (z0, x0) in zip(chunks, state):
        f0 = count[0]
        finish_forward(x0, [z0, z0 + 1, z0 + 2], mine)
        forwards.append(f0)
    for (copies, own, recv, mine, other), (z0, x0), f0 in zip(chunks, state, forwards):
        for e, s in enumerate([x0, f0, f0 + 1, f0 + 2]):
            landed((None, send_sem.at[s], recv_sem.at[s]), other.at[zsrc[e]])
    for c in started:
        c.wait_send()


def fused(queries, answer_keys, answer_values, prompt_keys, prompt_values, out_grad, block_counts, n):
    length, hd = queries.shape
    shard = prompt_keys.shape[0]
    keys = n * shard + length
    half = length // 2
    quarter = half // QUAD
    piece = shard // QUAD
    bf, f32 = jnp.bfloat16, jnp.float32
    sems = 4 * (n - 1) + 2 + 1 + 3 * (3 + 3 + 4)
    vmem = pl.BlockSpec(memory_space=pltpu.VMEM)
    return pl.pallas_call(
        functools.partial(kernel, n),
        out_shape=(
            jax.ShapeDtypeStruct((length, hd), bf),
            jax.ShapeDtypeStruct((length, hd), bf),
            jax.ShapeDtypeStruct((2, QUAD, piece, hd), bf),
            jax.ShapeDtypeStruct((2, 2, QUAD, quarter, hd), bf),
        ),
        in_specs=[vmem] * 6 + [pl.BlockSpec(memory_space=pltpu.SMEM)],
        out_specs=(vmem,) * 4,
        scratch_shapes=[
            pltpu.VMEM((keys, hd), bf),
            pltpu.VMEM((keys, hd), bf),
            pltpu.VMEM((length, hd), bf),
            pltpu.VMEM((keys, length), f32),
            pltpu.VMEM((keys, length), bf),
            pltpu.VMEM((keys, length), bf),
            pltpu.VMEM((2, shard, hd), f32),
            pltpu.VMEM((2, n - 1, shard, hd), bf),
            pltpu.VMEM((2, n - 1, shard, hd), bf),
            pltpu.VMEM((2, 2, half, hd), f32),
            pltpu.VMEM((2, 2, half, hd), bf),
            pltpu.VMEM((2, half, hd), bf),
            pltpu.VMEM((2, shard, hd), f32),
            pltpu.VMEM((2, shard, hd), bf),
            pltpu.VMEM((shard, hd), bf),
            pltpu.VMEM((QUAD, piece, hd), f32),
            pltpu.VMEM((QUAD, piece, hd), bf),
            pltpu.VMEM((QUAD - 1, piece, hd), bf),
            pltpu.VMEM((2, QUAD, quarter, hd), f32),
            pltpu.VMEM((2, QUAD, quarter, hd), bf),
            pltpu.VMEM((2, QUAD - 1, quarter, hd), bf),
            pltpu.SemaphoreType.DMA((sems,)),
            pltpu.SemaphoreType.DMA((sems,)),
        ],
        compiler_params=pltpu.CompilerParams(
            collective_id=0, has_side_effects=True, vmem_limit_bytes=48 * 1024 * 1024
        ),
    )(queries, answer_keys, answer_values, prompt_keys, prompt_values, out_grad, block_counts)


def shards(n, groups, queries, answer_keys, answer_values, prompt_keys, prompt_values, out_grad, block_counts):
    hd = queries.shape[2]
    length = queries.shape[1]
    shard = prompt_keys.shape[0]
    kv = [answer_keys[0], answer_values[0], prompt_keys, prompt_values]
    if groups > 1:
        kv_group = lax.axis_index("tp") // GROUP
        kv = [lax.dynamic_slice_in_dim(x, kv_group * hd, hd, 1) for x in kv]
    attended, query_grad, gp, ga = fused(queries[0], *kv, out_grad[0], block_counts, n)
    outs = [gp[0].reshape(shard, hd), gp[1].reshape(shard, hd), ga[0].reshape(length, hd), ga[1].reshape(length, hd)]
    if groups > 1:
        sets = [[g * GROUP + i for g in range(groups)] for i in range(GROUP)]
        outs = [lax.all_gather(x, "tp", axis=1, tiled=True, axis_index_groups=sets) for x in outs]
    return attended[None], query_grad[None], outs[0], outs[1], outs[2][None], outs[3][None]


def solution(mesh):
    n, tp = mesh.shape["comp"], mesh.shape["tp"]
    return jax.shard_map(
        functools.partial(shards, n, tp // GROUP),
        mesh=mesh,
        in_specs=(
            P("comp", None, "tp"),
            P("comp", None, None),
            P("comp", None, None),
            P("comp", None),
            P("comp", None),
            P("comp", None, "tp"),
            P(),
        ),
        out_specs=(
            P("comp", None, "tp"),
            P("comp", None, "tp"),
            P("comp", None),
            P("comp", None),
            P("comp", None, None),
            P("comp", None, None),
        ),
        check_vma=False,
    )
```

time: 119 us -> 41.1 us (0.35)
  blocking collectives: 58.1 us -> 0 us
  waiting for transfers between devices: 31.8 us -> 0 us
  Pallas kernels: 0 us -> 31.6 us
  between operations: 14.3 us -> 0.66 us
  matrix products: 9.72 us -> 0 us
  local copies, waits for them, and re-layouts: 1.92 us -> 8.53 us
  other arithmetic: 3.22 us -> 0 us
    psum x1 -> x0, blocking collectives: 45.4 us -> none  [shards(): lax.psum((embed_head(key_part), embed_head(value_term), embed_head(answer...]
    reduce_scatter x2 -> x0, waiting for transfers between devices: 31.8 us -> none  [the longest x1 23.4 us: shards(): lax.psum_scatter(prompt_terms[0], 'comp', scatter_dimension=0, tiled=True)]
    pallas_call x0 -> x1, Pallas kernels: none -> 31.6 us  [fused(): pl.pallas_call(functools.partial(kernel, n), out_shape=(jax.ShapeDtypeStr...]
    all_gather x2 -> x0, blocking collectives: 12.7 us -> none  [the longest x1 7.08 us: shards(): lax.all_gather(key_mine, 'comp', axis=0, tiled=True)]
    dot_general x12 -> x0, matrix products: 9.72 us -> none  [the longest x8 6.77 us: contract(): lax.dot_general(left, right, (((left_dim,), (right_dim,)), ((), ())), pre...]
    unnamed x24 -> x16, local copies, waits for them, and re-layouts: 1.92 us -> 7.17 us
    reduce_sum x3 -> x0, other arithmetic: 1.91 us -> none  [the longest x1 1.32 us: shards(): jnp.sum(jnp.where(jnp.arange(completions) == comp_index, row_counts, 0))]
    slice x0 -> x2, local copies, waits for them, and re-layouts: none -> 1.36 us  [the longest x1 0.71 us: shards(): ga[1].reshape(length, hd)]
  transfers between devices with their start and end apart: 2 -> 0, of which waited for: 2 -> 0; matrix products, arithmetic and copies ran while one was open for 7% -> 0% of each run, Pallas kernels for 0% -> 0%
where the time goes in v1:
time: 41.1 us; the launch traced here: 40.8 us
  Pallas kernels  31.6 us (77%)
  local copies, waits for them, and re-layouts  8.53 us (21%)
  between operations  0.66 us (2%)
    pallas_call x1, Pallas kernels, fused(): pl.pallas_call(functools.partial(kernel, n), out_shape=(jax.ShapeDtypeStr...  31.6 us
    unnamed x16, local copies, waits for them, and re-layouts  7.17 us

profile of v1, /device:TPU:0, one launch (start us, length us, event | category | flops | bytes accessed | tf_op | source)
XLA Modules:
  0.0 40.8 jit_solution(10995206879177174301)
XLA Ops:
  0.6 0.0 copy-start.6
  0.6 0.6 %copy-done.6 = s32[4]{0:T(128)S(1)} copy-done((s32[4]{0:T(128)S(1)}, s32[4]{0:T(128)}, u32[]{:S(2)}) %copy-start.6) | copy-done | bytes 40
  1.3 0.0 copy-start
  1.3 0.9 %copy-done = bf16[1,512,128]{2,1,0:T(8,128)(2,1)S(1)} copy-done((bf16[1,512,128]{2,1,0:T(8,128)(2,1)S(1)}, bf16[1,512,128]{2,1,0:T(8,128)(2,1)}, u32[]{:S(2)}) %copy-start) | copy-done | bytes 131096
  2.2 0.0 copy-start.1
  2.2 0.9 %copy-done.1 = bf16[1,512,128]{2,1,0:T(8,128)(2,1)S(1)} copy-done((bf16[1,512,128]{2,1,0:T(8,128)(2,1)S(1)}, bf16[1,512,128]{2,1,0:T(8,128)(2,1)}, u32[]{:S(2)}) %copy-start.1) | copy-done | bytes 131096
  3.1 0.0 copy-start.2
  3.1 0.9 %copy-done.2 = bf16[1,512,128]{2,1,0:T(8,128)(2,1)S(1)} copy-done((bf16[1,512,128]{2,1,0:T(8,128)(2,1)S(1)}, bf16[1,512,128]{2,1,0:T(8,128)(2,1)}, u32[]{:S(2)}) %copy-start.2) | copy-done | bytes 131096
  4.0 0.0 copy-start.3
  4.0 0.9 %copy-done.3 = bf16[1,512,128]{2,1,0:T(8,128)(2,1)S(1)} copy-done((bf16[1,512,128]{2,1,0:T(8,128)(2,1)S(1)}, bf16[1,512,128]{2,1,0:T(8,128)(2,1)}, u32[]{:S(2)}) %copy-start.3) | copy-done | bytes 131096
  4.9 0.0 copy-start.4
  4.9 0.8 %copy-done.4 = bf16[192,128]{1,0:T(8,128)(2,1)S(1)} copy-done((bf16[192,128]{1,0:T(8,128)(2,1)S(1)}, bf16[192,128]{1,0:T(8,128)(2,1)}, u32[]{:S(2)}) %copy-start.4) | copy-done | bytes 49176
  5.7 0.0 copy-start.5
  5.7 0.8 %copy-done.5 = bf16[192,128]{1,0:T(8,128)(2,1)S(1)} copy-done((bf16[192,128]{1,0:T(8,128)(2,1)S(1)}, bf16[192,128]{1,0:T(8,128)(2,1)}, u32[]{:S(2)}) %copy-start.5) | copy-done | bytes 49176
  6.5 31.6 %shard_map.118 = (bf16[512,128]{1,0:T(8,128)(2,1)S(1)}, bf16[512,128]{1,0:T(8,128)(2,1)S(1)}, bf16[2,4,48,128]{3,2,1,0:T(8,128)(2,1)S(1)}, bf16[2,2,4,64,128]{4,3,2,1,0:T(8,128)(2,1)S(1)}) custom-call(bf16[512,128]{1,0:T(8,128)(2,1)S(1)} %bitcast.12, bf16[512,128]{1,0:T(8,128)(2,1)S(1)} %bitcast.13, bf16[512,128]{1,0:T(8,128)(2,1)S(1)} %bitcast.14, ...), custom_call_target="tpu_custom_call" | custom-call | tf_op jit(solution)/shard_map/pallas_call | solution.py:276
  38.1 0.6 %fusion.1 = (bf16[1,4,48,128]{3,2,1,0:T(8,128)(2,1)}, bf16[1,4,48,128]{3,2,1,0:T(8,128)(2,1)}) fusion(bf16[2,4,48,128]{3,2,1,0:T(8,128)(2,1)S(1)} %get-tuple-element.12), kind=kLoop, calls=%fused_computation.1 | loop fusion | bytes 196608 | tf_op jit(solution)/shard_map/slice | solution.py:326
  38.8 0.7 %fusion = (bf16[1,2,4,64,128]{4,3,2,1,0:T(8,128)(2,1)}, bf16[1,2,4,64,128]{4,3,2,1,0:T(8,128)(2,1)}) fusion(bf16[2,2,4,64,128]{4,3,2,1,0:T(8,128)(2,1)S(1)} %get-tuple-element.13), kind=kLoop, calls=%fused_computation | loop fusion | bytes 524288 | tf_op jit(solution)/shard_map/slice | solution.py:326
  39.5 0.7 %copy.15 = bf16[1,512,128]{2,1,0:T(8,128)(2,1)} copy(bf16[1,512,128]{2,1,0:T(8,128)(2,1)S(1)} %bitcast.11) | data formatting | bytes 262144
  40.1 0.7 %copy.16 = bf16[1,512,128]{2,1,0:T(8,128)(2,1)} copy(bf16[1,512,128]{2,1,0:T(8,128)(2,1)S(1)} %bitcast.10) | data formatting | bytes 262144
Async XLA Ops:
  0.6 0.7 %copy-start.6 = (s32[4]{0:T(128)S(1)}, s32[4]{0:T(128)}, u32[]{:S(2)}) copy-start(s32[4]{0:T(128)} %cnt_ref.1) | copy-start | bytes 52
  1.3 0.9 %copy-start = (bf16[1,512,128]{2,1,0:T(8,128)(2,1)S(1)}, bf16[1,512,128]{2,1,0:T(8,128)(2,1)}, u32[]{:S(2)}) copy-start(bf16[1,512,128]{2,1,0:T(8,128)(2,1)} %param.7) | copy-start | bytes 393220
  2.2 0.9 %copy-start.1 = (bf16[1,512,128]{2,1,0:T(8,128)(2,1)S(1)}, bf16[1,512,128]{2,1,0:T(8,128)(2,1)}, u32[]{:S(2)}) copy-start(bf16[1,512,128]{2,1,0:T(8,128)(2,1)} %param.8) | copy-start | bytes 393220
  3.1 0.9 %copy-start.2 = (bf16[1,512,128]{2,1,0:T(8,128)(2,1)S(1)}, bf16[1,512,128]{2,1,0:T(8,128)(2,1)}, u32[]{:S(2)}) copy-start(bf16[1,512,128]{2,1,0:T(8,128)(2,1)} %param.9) | copy-start | bytes 393220
  4.0 0.9 %copy-start.3 = (bf16[1,512,128]{2,1,0:T(8,128)(2,1)S(1)}, bf16[1,512,128]{2,1,0:T(8,128)(2,1)}, u32[]{:S(2)}) copy-start(bf16[1,512,128]{2,1,0:T(8,128)(2,1)} %param.12) | copy-start | bytes 393220
  4.9 0.8 %copy-start.4 = (bf16[192,128]{1,0:T(8,128)(2,1)S(1)}, bf16[192,128]{1,0:T(8,128)(2,1)}, u32[]{:S(2)}) copy-start(bf16[192,128]{1,0:T(8,128)(2,1)} %kp_ref.1) | copy-start | bytes 147460
  5.7 0.8 %copy-start.5 = (bf16[192,128]{1,0:T(8,128)(2,1)S(1)}, bf16[192,128]{1,0:T(8,128)(2,1)}, u32[]{:S(2)}) copy-start(bf16[192,128]{1,0:T(8,128)(2,1)} %vp_ref.1) | copy-start | bytes 147460

commit v2 on v1

v2 whole, which is shorter than its diff:
```python
import functools
import jax
import jax.numpy as jnp
from jax import lax
from jax.experimental import pallas as pl
from jax.experimental.pallas import tpu as pltpu
from jax.sharding import PartitionSpec as P

GROUP = 8
BLK = 64
QUAD = 4
COLS = 256
NEG = -1e30
VMEM = 60 * 1024 * 1024
MESH = pl.DeviceIdType.MESH


def contract(left, right, left_dim, right_dim):
    return lax.dot_general(
        left, right, (((left_dim,), (right_dim,)), ((), ())), preferred_element_type=jnp.float32
    )


def kernel(
    n, q_in, ka_in, va_in, kp_in, vp_in, do_in, cnt_in,
    att_out, dq_out, gp_out, ga_out,
    att_ref, dq_ref, gp_ref, ga_ref, gp_own, ga_own, q_ref, do_ref, cnt_ref, k_all, v_all, do_m, st, pb, dsb,
    nsend, nrecv, pown, psend, precv, aown, asend, arecv,
    pzown, pzsend, pzrecv,
    send_sem, recv_sem, load_sem,
):
    me = lax.axis_index("comp")
    tp = lax.axis_index("tp")
    local = lax.rem(tp, GROUP)
    base = tp - local
    length, hd = q_ref.shape
    shard = kp_in.shape[0]
    prompt = n * shard
    factor = hd ** (-0.5)
    blocks = length // COLS
    chips = n // 2
    core = lax.rem(me, 2)
    sibling = {"comp": me + 1 - 2 * core}
    chip_to = [None] + [{"comp": lax.rem(me + 2 * d, n)} for d in range(1, chips)]
    chip_back = [None] + [{"comp": lax.rem(me + n - 2 * d, n)} for d in range(1, chips)]
    octet = [None] + [{"tp": base + lax.rem(local + e, GROUP)} for e in range(1, GROUP)]

    barrier = pltpu.get_barrier_semaphore()
    peers = chip_to[1:] + [sibling] + octet[1:]
    for peer in peers:
        pl.semaphore_signal(barrier, inc=1, device_id=peer, device_id_type=MESH)

    loads = []
    for s, (src, dst) in enumerate((
        (kp_in, k_all.at[pl.ds(0, shard)]), (vp_in, v_all.at[pl.ds(0, shard)]),
        (ka_in, k_all.at[pl.ds(prompt, length)]), (q_in, q_ref), (cnt_in, cnt_ref), (do_in, do_ref),
        (va_in, v_all.at[pl.ds(prompt, length)]),
    )):
        loads.append(pltpu.make_async_copy(src, dst, load_sem.at[s]))
        loads[-1].start()

    count = [0]
    started = []

    def copy(src, dst, device):
        s = count[0]
        count[0] += 1
        c = pltpu.make_async_remote_copy(
            src_ref=src, dst_ref=dst, send_sem=send_sem.at[s], recv_sem=recv_sem.at[s],
            device_id=device, device_id_type=MESH,
        )
        started.append(c)
        return c

    pl.semaphore_wait(barrier, len(peers))

    def slot(ref, d, other):
        return ref.at[pl.ds((2 * d + other) * shard, shard)]

    def spread(ref):
        near = copy(slot(ref, 0, 0), slot(ref, 0, 1), sibling)
        far = [copy(slot(ref, 0, 0), slot(ref, d, 0), chip_to[d]) for d in range(1, chips)]
        for c in far + [near]:
            c.start()
        return near, far

    loads[0].wait()
    k_in = spread(k_all)
    loads[1].wait()
    v_in = spread(v_all)

    def forward(ref, far, d):
        far[d - 1].wait_recv()
        c = copy(slot(ref, d, 0), slot(ref, d, 1), sibling)
        c.start()
        return c

    def cols(b):
        return slice(b * COLS, (b + 1) * COLS)

    def spans(b):
        return [(d * shard, shard) for d in range(n)] + [(prompt + a * COLS, COLS) for a in range(b + 1)]

    peaks = [None] * blocks

    def scores(b, at, size):
        s = contract(k_all[at:at + size], q_ref[cols(b)], 1, 1) * factor
        if at == prompt + b * COLS:
            m = lax.broadcasted_iota(jnp.int32, s.shape, 0)
            i = lax.broadcasted_iota(jnp.int32, s.shape, 1)
            s = jnp.where(m <= i, s, NEG)
        st[at:at + size, cols(b)] = s
        top = jnp.max(s, axis=0, keepdims=True)
        peaks[b] = top if peaks[b] is None else jnp.maximum(peaks[b], top)

    for c in loads[2:4]:
        c.wait()
    for b in range(blocks):
        for a in range(b + 1):
            scores(b, prompt + a * COLS, COLS)
        scores(b, 0, shard)
    for c in loads[4:]:
        c.wait()
    own_count = cnt_ref[me] * BLK
    row = lax.broadcasted_iota(jnp.int32, (length, hd), 0)
    do_m[...] = jnp.where(row < own_count, do_ref[...].astype(jnp.float32), 0.0).astype(jnp.bfloat16)
    k_in[0].wait_recv()
    for b in range(blocks):
        scores(b, shard, shard)
    k_fwd = [forward(k_all, k_in[1], d) for d in range(1, chips)]
    for d in range(1, chips):
        for b in range(blocks):
            scores(b, 2 * d * shard, shard)
    v_fwd = [forward(v_all, v_in[1], d) for d in range(1, chips)]
    for d in range(1, chips):
        k_fwd[d - 1].wait_recv()
        for b in range(blocks):
            scores(b, (2 * d + 1) * shard, shard)

    for b in range(blocks):
        total = jnp.zeros((1, COLS), jnp.float32)
        for at, size in spans(b):
            e = jnp.exp(st[at:at + size, cols(b)] - peaks[b])
            st[at:at + size, cols(b)] = e
            total = total + jnp.sum(e, axis=0, keepdims=True)
        inv = 1.0 / total
        for at, size in spans(b):
            p = st[at:at + size, cols(b)] * inv
            st[at:at + size, cols(b)] = p
            pb[at:at + size, cols(b)] = p.astype(jnp.bfloat16)

    p_near, p_far = [None, None], [None, None]

    def prompt_terms(w, probs, right):
        for slot_i in [2 * d + 1 for d in range(chips)] + [2 * d for d in range(chips)]:
            g = jnp.dot(
                probs[slot_i * shard:(slot_i + 1) * shard], right[...], preferred_element_type=jnp.float32
            )
            if slot_i % 2:
                nsend[w, slot_i // 2] = g.astype(jnp.bfloat16)
                if slot_i // 2 == chips - 1:
                    p_near[w] = copy(nsend.at[w], nrecv.at[w], sibling)
                    p_near[w].start()
            else:
                pown[w, slot_i // 2] = g

    def prompt_far(w):
        p_near[w].wait_recv()
        p_far[w] = []
        for d in range(1, chips):
            psend[w, d - 1] = (pown[w, d] + nrecv[w, d].astype(jnp.float32)).astype(jnp.bfloat16)
            p_far[w].append(copy(psend.at[w, d - 1], precv.at[w, d - 1], chip_back[d]))
            p_far[w][-1].start()

    def octet_scatter(send, recv, place):
        out = []
        for e in range(1, GROUP):
            out.append(copy(send.at[place(lax.rem(local + e, GROUP))], recv.at[e - 1], octet[e]))
            out[-1].start()
        return out

    def octet_gather(copies, own, recv, stage, out, place):
        total = own[place(local)]
        for e in range(1, GROUP):
            copies[e - 1].wait_recv()
            total = total + recv[e - 1].astype(jnp.float32)
        stage[...] = total.astype(jnp.bfloat16)
        first = count[0]
        for e in range(1, GROUP):
            copy(stage, out.at[place(local)], octet[e]).start()
        out[place(local)] = total.astype(jnp.bfloat16)
        return first

    def octet_finish(first, out, place):
        for e in range(1, GROUP):
            ref = out.at[place(lax.rem(local + GROUP - e, GROUP))]
            pltpu.make_async_remote_copy(
                src_ref=ref, dst_ref=ref, send_sem=send_sem.at[first + e - 1], recv_sem=recv_sem.at[first + e - 1],
                device_id=octet[e], device_id_type=MESH,
            ).wait_recv()

    def straight(member):
        return member

    def paired(member):
        return lax.rem(member, 2) * QUAD + member // 2

    eighth = length // GROUP

    def answer_terms(w, probs, right):
        for a in range(blocks):
            at = prompt + a * COLS
            g = jnp.dot(
                probs[at:at + COLS, a * COLS:], right[a * COLS:], preferred_element_type=jnp.float32
            ).reshape(COLS // eighth, eighth, hd)
            first = a * COLS // eighth
            aown[w, first:first + COLS // eighth] = g
            asend[w, first:first + COLS // eighth] = g.astype(jnp.bfloat16)
        return octet_scatter(asend.at[w], arecv.at[w], straight)

    prompt_terms(1, pb, do_m)
    av = answer_terms(1, pb, do_m)

    prompt_far(1)
    for c in [v_in[0]] + v_fwd:
        c.wait_recv()
    stores = []

    def keep(src, dst):
        stores.append(pltpu.make_async_copy(src, dst, load_sem.at[7 + len(stores)]))
        stores[-1].start()

    deltas = []
    for b in range(blocks):
        keys = prompt + (b + 1) * COLS
        mixed = contract(v_all[:keys], pb[:keys, cols(b)], 0, 0)
        lane = lax.broadcasted_iota(jnp.int32, mixed.shape, 1) + b * COLS
        mixed = jnp.where(lane < own_count, mixed, 0.0).astype(jnp.bfloat16).astype(jnp.float32)
        att_ref[cols(b)] = mixed.T.astype(jnp.bfloat16)
        dout_t = do_m[cols(b)].astype(jnp.float32).T
        deltas.append(jnp.sum(dout_t * mixed, axis=0, keepdims=True))

    keep(att_ref, att_out)
    def score_grads(b, at, size):
        dp = contract(v_all[at:at + size], do_m[cols(b)], 1, 1)
        ds = st[at:at + size, cols(b)] * (dp - deltas[b]) * factor
        dsb[at:at + size, cols(b)] = ds.astype(jnp.bfloat16)

    for b in range(blocks):
        for at, size in spans(b)[:n]:
            score_grads(b, at, size)
    prompt_terms(0, dsb, q_ref)
    for b in range(blocks):
        for at, size in spans(b)[n:]:
            score_grads(b, at, size)
    ak = answer_terms(0, dsb, q_ref)
    prompt_far(0)
    av_out = octet_gather(av, aown.at[1], arecv.at[1], ga_own.at[1], ga_ref.at[1], straight)

    for b in range(blocks):
        keys = prompt + (b + 1) * COLS
        dq = contract(k_all[:keys], dsb[:keys, cols(b)], 0, 0)
        dq_ref[cols(b)] = dq.T.astype(jnp.bfloat16)
    keep(dq_ref, dq_out)

    for w in (1, 0):
        total = pown[w, 0] + nrecv[w, 0].astype(jnp.float32)
        for d in range(1, chips):
            p_far[w][d - 1].wait_recv()
            total = total + precv[w, d - 1].astype(jnp.float32)
        size = shard // QUAD
        for z in range(QUAD):
            pzown[w * QUAD + z] = total[z * size:(z + 1) * size]
            pzsend[w * QUAD + z] = total[z * size:(z + 1) * size].astype(jnp.bfloat16)

    ap = octet_scatter(pzsend, pzrecv, paired)
    ak_out = octet_gather(ak, aown.at[0], arecv.at[0], ga_own.at[0], ga_ref.at[0], straight)
    ap_out = octet_gather(ap, pzown, pzrecv, gp_own, gp_ref, paired)
    octet_finish(av_out, ga_ref.at[1], straight)
    keep(ga_ref.at[1], ga_out.at[1])
    octet_finish(ak_out, ga_ref.at[0], straight)
    keep(ga_ref.at[0], ga_out.at[0])
    octet_finish(ap_out, gp_ref, paired)
    keep(gp_ref, gp_out)
    for c in stores:
        c.wait()
    for c in started:
        c.wait_send()


def fused(queries, answer_keys, answer_values, prompt_keys, prompt_values, out_grad, block_counts, n):
    length, hd = queries.shape
    shard = prompt_keys.shape[0]
    keys = n * shard + length
    eighth = length // GROUP
    piece = shard // QUAD
    bf, f32 = jnp.bfloat16, jnp.float32
    chips = n // 2
    sems = 2 * (2 * chips - 1) + 2 * chips + 6 * (GROUP - 1)
    hbm = pl.BlockSpec(memory_space=pl.ANY)
    return pl.pallas_call(
        functools.partial(kernel, n),
        out_shape=(
            jax.ShapeDtypeStruct((length, hd), bf),
            jax.ShapeDtypeStruct((length, hd), bf),
            jax.ShapeDtypeStruct((GROUP, piece, hd), bf),
            jax.ShapeDtypeStruct((2, GROUP, eighth, hd), bf),
        ),
        in_specs=[hbm] * 7,
        out_specs=(hbm,) * 4,
        scratch_shapes=[
            pltpu.VMEM((length, hd), bf),
            pltpu.VMEM((length, hd), bf),
            pltpu.VMEM((GROUP, piece, hd), bf),
            pltpu.VMEM((2, GROUP, eighth, hd), bf),
            pltpu.VMEM((piece, hd), bf),
            pltpu.VMEM((2, eighth, hd), bf),
            pltpu.VMEM((length, hd), bf),
            pltpu.VMEM((length, hd), bf),
            pltpu.SMEM(block_counts.shape, jnp.int32),
            pltpu.VMEM((keys, hd), bf),
            pltpu.VMEM((keys, hd), bf),
            pltpu.VMEM((length, hd), bf),
            pltpu.VMEM((keys, length), f32),
            pltpu.VMEM((keys, length), bf),
            pltpu.VMEM((keys, length), bf),
            pltpu.VMEM((2, chips, shard, hd), bf),
            pltpu.VMEM((2, chips, shard, hd), bf),
            pltpu.VMEM((2, chips, shard, hd), f32),
            pltpu.VMEM((2, chips - 1, shard, hd), bf),
            pltpu.VMEM((2, chips - 1, shard, hd), bf),
            pltpu.VMEM((2, GROUP, eighth, hd), f32),
            pltpu.VMEM((2, GROUP, eighth, hd), bf),
            pltpu.VMEM((2, GROUP - 1, eighth, hd), bf),
            pltpu.VMEM((GROUP, piece, hd), f32),
            pltpu.VMEM((GROUP, piece, hd), bf),
            pltpu.VMEM((GROUP - 1, piece, hd), bf),
            pltpu.SemaphoreType.DMA((sems,)),
            pltpu.SemaphoreType.DMA((sems,)),
            pltpu.SemaphoreType.DMA((12,)),
        ],
        compiler_params=pltpu.CompilerParams(
            collective_id=0, has_side_effects=True, vmem_limit_bytes=VMEM
        ),
    )(queries, answer_keys, answer_values, prompt_keys, prompt_values, out_grad, block_counts)


def store(att, dq, gp, ga, *refs):
    outs, held, load, save = refs[:6], refs[6:12], refs[12], refs[13]
    sources = (ga.at[0], ga.at[1], att, dq, gp.at[0], gp.at[1])
    copies = [
        (pltpu.make_async_copy(src, mid, load.at[s]), pltpu.make_async_copy(mid, dst, save.at[s]))
        for s, (src, mid, dst) in enumerate(zip(sources, held, outs))
    ]
    for c, _ in copies:
        c.start()
    for c, then in copies:
        c.wait()
        then.start()
    for _, c in copies:
        c.wait()


def write_out(att, dq, gp, ga):
    shapes = [jax.ShapeDtypeStruct(x.shape, x.dtype) for x in (ga[0], ga[1], att, dq, gp[0], gp[1])]
    results = pl.pallas_call(
        store,
        out_shape=shapes,
        in_specs=[pl.BlockSpec(memory_space=pl.ANY)] * 4,
        out_specs=[pl.BlockSpec(memory_space=pl.ANY)] * 6,
        scratch_shapes=[pltpu.VMEM(x.shape, x.dtype) for x in shapes]
        + [pltpu.SemaphoreType.DMA((6,)), pltpu.SemaphoreType.DMA((6,))],
        compiler_params=pltpu.CompilerParams(vmem_limit_bytes=VMEM),
    )(att, dq, gp, ga)
    return results[2], results[3], results[4:], results[:2]


def shards(n, groups, queries, answer_keys, answer_values, prompt_keys, prompt_values, out_grad, block_counts):
    hd = queries.shape[2]
    length = queries.shape[1]
    shard = prompt_keys.shape[0]
    kv = [answer_keys[0], answer_values[0], prompt_keys, prompt_values]
    if groups > 1:
        kv_group = lax.axis_index("tp") // GROUP
        kv = [lax.dynamic_slice_in_dim(x, kv_group * hd, hd, 1) for x in kv]
    attended, query_grad, gp, ga = fused(queries[0], *kv, out_grad[0], block_counts, n)
    gp = gp.reshape(2, shard, hd)
    attended, query_grad, gp, ga = write_out(attended, query_grad, gp, ga)
    outs = [gp[0].reshape(shard, hd), gp[1].reshape(shard, hd), ga[0].reshape(length, hd), ga[1].reshape(length, hd)]
    if groups > 1:
        sets = [[g * GROUP + i for g in range(groups)] for i in range(GROUP)]
        outs = [lax.all_gather(x, "tp", axis=1, tiled=True, axis_index_groups=sets) for x in outs]
    return attended[None], query_grad[None], outs[0], outs[1], outs[2][None], outs[3][None]


def solution(mesh):
    n, tp = mesh.shape["comp"], mesh.shape["tp"]
    return jax.shard_map(
        functools.partial(shards, n, tp // GROUP),
        mesh=mesh,
        in_specs=(
            P("comp", None, "tp"),
            P("comp", None, None),
            P("comp", None, None),
            P("comp", None),
            P("comp", None),
            P("comp", None, "tp"),
            P(),
        ),
        out_specs=(
            P("comp", None, "tp"),
            P("comp", None, "tp"),
            P("comp", None),
            P("comp", None),
            P("comp", None, None),
            P("comp", None, None),
        ),
        check_vma=False,
    )
```

time: 41.1 us -> 35 us (0.85)
  local copies, waits for them, and re-layouts: 8.53 us -> 0 us
  Pallas kernels: 31.6 us -> 34.2 us
    unnamed x16 -> x0, local copies, waits for them, and re-layouts: 7.17 us -> none
    pallas_call x0 -> x1, Pallas kernels: none -> 1.88 us  [write_out(): pl.pallas_call(store, out_shape=shapes, in_specs=[pl.BlockSpec(memory_spa...]
    slice x2 -> x0, local copies, waits for them, and re-layouts: 1.36 us -> none  [the longest x1 0.71 us: shards(): ga[1].reshape(length, hd)]
    pallas_call x1, Pallas kernels: 31.6 us -> 32.3 us  [fused(): pl.pallas_call(functools.partial(kernel, n), out_shape=(jax.ShapeDtypeStr...]
where the time goes in v2:
time: 35 us; the launch traced here: 34.9 us
  Pallas kernels  34.2 us (98%)
  between operations  0.64 us (2%)
    pallas_call x1, Pallas kernels, fused(): pl.pallas_call(functools.partial(kernel, n), out_shape=(jax.ShapeDtypeStr...  32.3 us
    pallas_call x1, Pallas kernels, write_out(): pl.pallas_call(store, out_shape=shapes, in_specs=[pl.BlockSpec(memory_spa...  1.88 us

profile of v2, /device:TPU:0, one launch (start us, length us, event | category | flops | bytes accessed | tf_op | source)
XLA Modules:
  0.0 34.9 jit_solution(814744105395679804)
XLA Ops:
  0.6 32.3 %shard_map.118 = (bf16[512,128]{1,0:T(8,128)(2,1)}, bf16[512,128]{1,0:T(8,128)(2,1)}, bf16[8,48,128]{2,1,0:T(8,128)(2,1)}, bf16[2,8,64,128]{3,2,1,0:T(8,128)(2,1)}) custom-call(bf16[512,128]{1,0:T(8,128)(2,1)} %bitcast.9, bf16[512,128]{1,0:T(8,128)(2,1)} %bitcast.10, bf16[512,128]{1,0:T(8,128)(2,1)} %bitcast.11, bf16[192,128]{1,0:T(8,128)(2,1)} %kp_in.1, ...), custom_call_target="tpu_custom_call" | custom-call | tf_op jit(solution)/shard_map/pallas_call | solution.py:301
  33.0 1.9 %shard_map.119 = (bf16[8,64,128]{2,1,0:T(8,128)(2,1)}, bf16[8,64,128]{2,1,0:T(8,128)(2,1)}, bf16[512,128]{1,0:T(8,128)(2,1)}, bf16[512,128]{1,0:T(8,128)(2,1)}, ...) custom-call(bf16[512,128]{1,0:T(8,128)(2,1)} %get-tuple-element.16.att, bf16[512,128]{1,0:T(8,128)(2,1)} %get-tuple-element.17.dq, ...), custom_call_target="tpu_custom_call" | custom-call | tf_op jit(solution)/shard_map/pallas_call | solution.py:366

commit v3 on v2

--- a/solution.py
+++ b/solution.py
@@ -33,6 +33,8 @@
     tp = lax.axis_index("tp")
     local = lax.rem(tp, GROUP)
     base = tp - local
+    other = local + 1 - 2 * lax.rem(local, 2)
+    partner = {"tp": base + other}
     length, hd = q_ref.shape
     shard = kp_in.shape[0]
     prompt = n * shard
@@ -199,6 +201,38 @@
                 device_id=octet[e], device_id_type=MESH,
             ).wait_recv()
 
+    def relay_gather(copies, own, recv, stage, out):
+        total = own[local]
+        for e in range(1, GROUP):
+            copies[e - 1].wait_recv()
+            total = total + recv[e - 1].astype(jnp.float32)
+        stage[...] = total.astype(jnp.bfloat16)
+        first = count[0]
+        for e in range(2, GROUP, 2):
+            copy(stage, out.at[local], octet[e]).start()
+        copy(stage, out.at[local], partner).start()
+        out[local] = total.astype(jnp.bfloat16)
+        return first
+
+    def arrived(s, ref):
+        pltpu.make_async_remote_copy(
+            src_ref=ref, dst_ref=ref, send_sem=send_sem.at[s], recv_sem=recv_sem.at[s],
+            device_id=partner, device_id_type=MESH,
+        ).wait_recv()
+
+    def relay_forward(first, out):
+        passed = [first + QUAD - 1]
+        for z in range(1, QUAD):
+            piece = out.at[lax.rem(local + GROUP - 2 * z, GROUP)]
+            arrived(first + z - 1, piece)
+            passed.append(count[0])
+            copy(piece, piece, partner).start()
+        return passed
+
+    def relay_finish(passed, out):
+        for z in range(QUAD):
+            arrived(passed[z], out.at[lax.rem(other + GROUP - 2 * z, GROUP)])
+
     def straight(member):
         return member
 
@@ -253,9 +287,9 @@
     for b in range(blocks):
         for at, size in spans(b)[n:]:
             score_grads(b, at, size)
+    prompt_far(0)
     ak = answer_terms(0, dsb, q_ref)
-    prompt_far(0)
-    av_out = octet_gather(av, aown.at[1], arecv.at[1], ga_own.at[1], ga_ref.at[1], straight)
+    av_out = relay_gather(av, aown.at[1], arecv.at[1], ga_own.at[1], ga_ref.at[1])
 
     for b in range(blocks):
         keys = prompt + (b + 1) * COLS
@@ -274,11 +308,13 @@
             pzsend[w * QUAD + z] = total[z * size:(z + 1) * size].astype(jnp.bfloat16)
 
     ap = octet_scatter(pzsend, pzrecv, paired)
-    ak_out = octet_gather(ak, aown.at[0], arecv.at[0], ga_own.at[0], ga_ref.at[0], straight)
+    av_out = relay_forward(av_out, ga_ref.at[1])
+    ak_out = relay_gather(ak, aown.at[0], arecv.at[0], ga_own.at[0], ga_ref.at[0])
     ap_out = octet_gather(ap, pzown, pzrecv, gp_own, gp_ref, paired)
-    octet_finish(av_out, ga_ref.at[1], straight)
+    ak_out = relay_forward(ak_out, ga_ref.at[0])
+    relay_finish(av_out, ga_ref.at[1])
     keep(ga_ref.at[1], ga_out.at[1])
-    octet_finish(ak_out, ga_ref.at[0], straight)
+    relay_finish(ak_out, ga_ref.at[0])
     keep(ga_ref.at[0], ga_out.at[0])
     octet_finish(ap_out, gp_ref, paired)
     keep(gp_ref, gp_out)

time: 35 us -> 32.7 us (0.934)
  Pallas kernels: 34.2 us -> 31.9 us
    pallas_call x1, Pallas kernels: 32.3 us -> 30 us  [fused(): pl.pallas_call(functools.partial(kernel, n), out_shape=(jax.ShapeDtypeStr...]
where the time goes in v3:
time: 32.7 us; the launch traced here: 32.6 us
  Pallas kernels  31.9 us (98%)
  between operations  0.64 us (2%)
    pallas_call x1, Pallas kernels, fused(): pl.pallas_call(functools.partial(kernel, n), out_shape=(jax.ShapeDtypeStr...  30 us
    pallas_call x1, Pallas kernels, write_out(): pl.pallas_call(store, out_shape=shapes, in_specs=[pl.BlockSpec(memory_spa...  1.88 us

profile of v3, /device:TPU:0, one launch (start us, length us, event | category | flops | bytes accessed | tf_op | source)
XLA Modules:
  0.0 32.6 jit_solution(4479549177924214839)
XLA Ops:
  0.6 30.0 %shard_map.118 = (bf16[512,128]{1,0:T(8,128)(2,1)}, bf16[512,128]{1,0:T(8,128)(2,1)}, bf16[8,48,128]{2,1,0:T(8,128)(2,1)}, bf16[2,8,64,128]{3,2,1,0:T(8,128)(2,1)}) custom-call(bf16[512,128]{1,0:T(8,128)(2,1)} %bitcast.9, bf16[512,128]{1,0:T(8,128)(2,1)} %bitcast.10, bf16[512,128]{1,0:T(8,128)(2,1)} %bitcast.11, bf16[192,128]{1,0:T(8,128)(2,1)} %kp_in.1, ...), custom_call_target="tpu_custom_call" | custom-call | tf_op jit(solution)/shard_map/pallas_call | solution.py:337
  30.7 1.9 %shard_map.119 = (bf16[8,64,128]{2,1,0:T(8,128)(2,1)}, bf16[8,64,128]{2,1,0:T(8,128)(2,1)}, bf16[512,128]{1,0:T(8,128)(2,1)}, bf16[512,128]{1,0:T(8,128)(2,1)}, ...) custom-call(bf16[512,128]{1,0:T(8,128)(2,1)} %get-tuple-element.16.att, bf16[512,128]{1,0:T(8,128)(2,1)} %get-tuple-element.17.dq, ...), custom_call_target="tpu_custom_call" | custom-call | tf_op jit(solution)/shard_map/pallas_call | solution.py:402

commit v4 on v3

--- a/solution.py
+++ b/solution.py
@@ -151,25 +151,24 @@
             st[at:at + size, cols(b)] = p
             pb[at:at + size, cols(b)] = p.astype(jnp.bfloat16)
 
-    p_near, p_far = [None, None], [None, None]
+    p_near, p_far = [[None] * chips, [None] * chips], [None, None]
 
     def prompt_terms(w, probs, right):
-        for slot_i in [2 * d + 1 for d in range(chips)] + [2 * d for d in range(chips)]:
+        for slot_i in [2 * d + 1 for d in reversed(range(chips))] + [2 * d for d in reversed(range(chips))]:
             g = jnp.dot(
                 probs[slot_i * shard:(slot_i + 1) * shard], right[...], preferred_element_type=jnp.float32
             )
             if slot_i % 2:
                 nsend[w, slot_i // 2] = g.astype(jnp.bfloat16)
-                if slot_i // 2 == chips - 1:
-                    p_near[w] = copy(nsend.at[w], nrecv.at[w], sibling)
-                    p_near[w].start()
+                p_near[w][slot_i // 2] = copy(nsend.at[w, slot_i // 2], nrecv.at[w, slot_i // 2], sibling)
+                p_near[w][slot_i // 2].start()
             else:
                 pown[w, slot_i // 2] = g
 
     def prompt_far(w):
-        p_near[w].wait_recv()
         p_far[w] = []
         for d in range(1, chips):
+            p_near[w][d].wait_recv()
             psend[w, d - 1] = (pown[w, d] + nrecv[w, d].astype(jnp.float32)).astype(jnp.bfloat16)
             p_far[w].append(copy(psend.at[w, d - 1], precv.at[w, d - 1], chip_back[d]))
             p_far[w][-1].start()
@@ -252,8 +251,8 @@
             asend[w, first:first + COLS // eighth] = g.astype(jnp.bfloat16)
         return octet_scatter(asend.at[w], arecv.at[w], straight)
 
+    av = answer_terms(1, pb, do_m)
     prompt_terms(1, pb, do_m)
-    av = answer_terms(1, pb, do_m)
 
     prompt_far(1)
     for c in [v_in[0]] + v_fwd:
@@ -298,6 +297,7 @@
     keep(dq_ref, dq_out)
 
     for w in (1, 0):
+        p_near[w][0].wait_recv()
         total = pown[w, 0] + nrecv[w, 0].astype(jnp.float32)
         for d in range(1, chips):
             p_far[w][d - 1].wait_recv()
@@ -332,7 +332,7 @@
     piece = shard // QUAD
     bf, f32 = jnp.bfloat16, jnp.float32
     chips = n // 2
-    sems = 2 * (2 * chips - 1) + 2 * chips + 6 * (GROUP - 1)
+    sems = 2 * (2 * chips - 1) + 2 * (2 * chips - 1) + 6 * (GROUP - 1)
     hbm = pl.BlockSpec(memory_space=pl.ANY)
     return pl.pallas_call(
         functools.partial(kernel, n),

time: 32.7 us -> 32.2 us (0.985)
  Pallas kernels: 31.9 us -> 31.4 us
    pallas_call x1, Pallas kernels: 30 us -> 29.5 us  [fused(): pl.pallas_call(functools.partial(kernel, n), out_shape=(jax.ShapeDtypeStr...]
where the time goes in v4:
time: 32.2 us; the launch traced here: 32.1 us
  Pallas kernels  31.4 us (98%)
  between operations  0.64 us (2%)
    pallas_call x1, Pallas kernels, fused(): pl.pallas_call(functools.partial(kernel, n), out_shape=(jax.ShapeDtypeStr...  29.5 us
    pallas_call x1, Pallas kernels, write_out(): pl.pallas_call(store, out_shape=shapes, in_specs=[pl.BlockSpec(memory_spa...  1.88 us

profile of v4, /device:TPU:0, one launch (start us, length us, event | category | flops | bytes accessed | tf_op | source)
XLA Modules:
  0.0 32.1 jit_solution(15320742710507274662)
XLA Ops:
  0.6 29.5 %shard_map.118 = (bf16[512,128]{1,0:T(8,128)(2,1)}, bf16[512,128]{1,0:T(8,128)(2,1)}, bf16[8,48,128]{2,1,0:T(8,128)(2,1)}, bf16[2,8,64,128]{3,2,1,0:T(8,128)(2,1)}) custom-call(bf16[512,128]{1,0:T(8,128)(2,1)} %bitcast.9, bf16[512,128]{1,0:T(8,128)(2,1)} %bitcast.10, bf16[512,128]{1,0:T(8,128)(2,1)} %bitcast.11, bf16[192,128]{1,0:T(8,128)(2,1)} %kp_in.1, ...), custom_call_target="tpu_custom_call" | custom-call | tf_op jit(solution)/shard_map/pallas_call | solution.py:337
  30.2 1.9 %shard_map.119 = (bf16[8,64,128]{2,1,0:T(8,128)(2,1)}, bf16[8,64,128]{2,1,0:T(8,128)(2,1)}, bf16[512,128]{1,0:T(8,128)(2,1)}, bf16[512,128]{1,0:T(8,128)(2,1)}, ...) custom-call(bf16[512,128]{1,0:T(8,128)(2,1)} %get-tuple-element.16.att, bf16[512,128]{1,0:T(8,128)(2,1)} %get-tuple-element.17.dq, ...), custom_call_target="tpu_custom_call" | custom-call | tf_op jit(solution)/shard_map/pallas_call | solution.py:402
